TPU v7x, 32 devices: a whole 2x2x4 slice. The times are simulated.
32 devices in a mesh: groups: 2 (over x), tensor: 16 (over z, y, core).
Axes of the slice: x: 2, y: 2, z: 4, core: 2. Of those that a mesh axis runs over, the one named last changes fastest.
Arguments:
- tokens: int32 [3, 32], P(None, 'groups'), parts along dimension 1, may hold values from 0 to 32767
- page_table: int32 [32, 2], P('groups'), parts along dimension 0, may hold values from 0 to 15, as said below
- embedding: bfloat16 [32768, 8192], P(None, 'tensor'), may hold values from -6 to 6
- norm_gain: float32 [8192], replicated, may hold values from 0.5 to 1.5
- x_weight: bfloat16 [8192, 16384], P(None, 'tensor'), may hold values from -0.0625 to 0.0625
- z_weight: bfloat16 [8192, 16384], P(None, 'tensor'), may hold values from -0.0625 to 0.0625
- conv_weight: float32 [4, 16384], P(None, 'tensor'), may hold values from -3 to 3
- conv_bias: float32 [16384], P('tensor'), may hold values from -3 to 3
- proj_weight: bfloat16 [16384, 544], P('tensor'), may hold values from -0.046875 to 0.046875
- delta_gain: float32 [512], replicated, may hold values from 0.5 to 1.5
- delta_weight: bfloat16 [512, 16384], P(None, 'tensor'), may hold values from -0.25 to 0.25
- delta_bias: float32 [16384], P('tensor'), may hold values from -5 to 0
- log_rates: float32 [16, 16384], P(None, 'tensor'), may hold values from -4 to 2.5
- skip_gain: float32 [16384], P('tensor'), may hold values from 0.5 to 2
- out_weight: bfloat16 [16384, 8192], P('tensor'), may hold values from -0.0625 to 0.0625
- ssm_pages: bfloat16 [32, 16, 16384], P(('groups', 'tensor')), parts along dimension 0, may hold values from -6 to 6
- conv_pages: bfloat16 [32, 3, 16384], P(('groups', 'tensor')), parts along dimension 0, may hold values from -6 to 6
Outputs:
- hidden_out: bfloat16 [3, 32, 8192], P(None, 'groups', 'tensor'), parts along dimension 1
- ssm_out: bfloat16 [32, 16, 16384], P(('groups', 'tensor')), parts along dimension 0
- conv_out: bfloat16 [32, 3, 16384], P(('groups', 'tensor')), parts along dimension 0
There are 2 independent parts, one for each index of `groups`. A program takes and returns all parts, laid end to end along the dimension named above; an argument that names none is the same for every part. Nothing has to cross between parts.
Inputs may be any that keep to these rules, and one draw needn't show every extreme that they name: `page_table`: column 0 is an owner index below 16, column 1 a slot below 1; every pair of owner and slot is named by exactly one row.
All inputs are finite; a program needn't handle non-finite values.
Results may differ from a plain program's by a relative error of at most 0.0068.
Values may be sent and summed in bfloat16 or wider, within the bound.
A program may use at most 256 MiB of HBM per device.

v0:
```python
import jax
import jax.numpy as jnp
from jax import lax
from jax.sharding import PartitionSpec as P


def body(
    tokens,
    page_table,
    embedding,
    norm_gain,
    x_weight,
    z_weight,
    conv_weight,
    conv_bias,
    proj_weight,
    delta_gain,
    delta_weight,
    delta_bias,
    log_rates,
    skip_gain,
    out_weight,
    ssm_pages,
    conv_pages,
):
    slot_count = ssm_pages.shape[0]
    low_rank = delta_weight.shape[0]
    state_width = log_rates.shape[0]
    step_count = tokens.shape[0]
    state_arrived, window_arrived = (
        lax.all_to_all(ssm_pages, "tensor", split_axis=2, concat_axis=0, tiled=True),
        lax.all_to_all(conv_pages, "tensor", split_axis=2, concat_axis=0, tiled=True),
    )
    page_index = page_table[:, 0] * slot_count + page_table[:, 1]
    ssm_state = state_arrived[page_index].astype(jnp.float32)
    window = window_arrived[page_index]
    local_rows = embedding[tokens]
    rates = -jnp.exp(log_rates)
    gated_list = []
    for position in range(step_count):
        gathered = lax.all_gather(local_rows[position], "tensor", axis=1, tiled=True)
        values = gathered.astype(jnp.float32)
        normed = (
            values
            * lax.rsqrt(jnp.mean(values * values, axis=-1, keepdims=True) + 1e-06)
            * norm_gain
        ).astype(jnp.bfloat16)
        x_inner = jnp.dot(normed, x_weight, preferred_element_type=jnp.float32).astype(jnp.bfloat16)
        z_inner = jnp.dot(normed, z_weight, preferred_element_type=jnp.float32)
        conv_input = jnp.concatenate([window, x_inner[:, None, :]], axis=1).astype(jnp.float32)
        conv_act = jax.nn.silu(jnp.sum(conv_input * conv_weight[None], axis=1) + conv_bias)
        conv_bf = conv_act.astype(jnp.bfloat16)
        partial_proj = jnp.dot(conv_bf, proj_weight, preferred_element_type=jnp.float32)
        projected = lax.psum(partial_proj, "tensor")
        delta_low = projected[:, :low_rank]
        input_mat = projected[:, low_rank : low_rank + state_width]
        output_mat = projected[:, low_rank + state_width :]
        delta_norm = (
            delta_low
            * lax.rsqrt(jnp.mean(delta_low * delta_low, axis=-1, keepdims=True) + 1e-06)
            * delta_gain
        ).astype(jnp.bfloat16)
        delta = jax.nn.softplus(
            jnp.dot(delta_norm, delta_weight, preferred_element_type=jnp.float32) + delta_bias
        )
        ssm_state = (
            ssm_state * jnp.exp(delta[:, None, :] * rates[None])
            + (delta * conv_act)[:, None, :] * input_mat[:, :, None]
        )
        readout = (
            jnp.sum(ssm_state * output_mat[:, :, None], axis=1) + skip_gain * conv_act
        ) * jax.nn.silu(z_inner)
        readout = readout.astype(jnp.bfloat16)
        gated_list.append(readout)
        window = jnp.concatenate([window[:, 1:], x_inner[:, None, :]], axis=1)
    gated = jnp.stack(gated_list)
    partial_all = jnp.einsum("src,cd->srd", gated, out_weight, preferred_element_type=jnp.float32)
    mixer_all = lax.psum_scatter(partial_all, "tensor", scatter_dimension=2, tiled=True)
    hidden_local = (local_rows.astype(jnp.float32) + mixer_all).astype(jnp.bfloat16)
    final_state = ssm_state.astype(jnp.bfloat16)
    state_back = jnp.zeros_like(final_state).at[page_index].set(final_state)
    window_back = jnp.zeros_like(window).at[page_index].set(window)
    ssm_out, conv_out = (
        lax.all_to_all(state_back, "tensor", split_axis=0, concat_axis=2, tiled=True),
        lax.all_to_all(window_back, "tensor", split_axis=0, concat_axis=2, tiled=True),
    )
    return (hidden_local, ssm_out, conv_out)


def solution(mesh):
    placed = (
        P(None, "groups"),
        P("groups", None),
        P(None, "tensor"),
        P(),
        P(None, "tensor"),
        P(None, "tensor"),
        P(None, "tensor"),
        P("tensor"),
        P("tensor", None),
        P(),
        P(None, "tensor"),
        P("tensor"),
        P(None, "tensor"),
        P("tensor"),
        P("tensor", None),
        P(("groups", "tensor"), None, None),
        P(("groups", "tensor"), None, None),
    )
    return jax.shard_map(
        body,
        mesh=mesh,
        in_specs=placed,
        out_specs=(
            P(None, "groups", "tensor"),
            P(("groups", "tensor"), None, None),
            P(("groups", "tensor"), None, None),
        ),
        check_vma=False,
    )
```

profile of v0, /device:TPU:0, one launch (start us, length us, event | category | flops | bytes accessed | tf_op | source)
XLA Modules:
  0.0 595.5 jit_solution(9129518718801886170)
XLA Ops:
  7.2 15.4 %copy.60 = bf16[1,3,16384]{1,0,2:T(2,128)(2,1)} copy(bf16[1,3,16384]{2,1,0:T(4,128)(2,1)} %param.33) | data formatting | bytes 196608 | tf_op args[16]
  23.2 90.8 %reduce = bf16[16384,3]{1,0:T(8,128)(2,1)} reduce(bf16[16384,1,3]{2,1,0:T(2,128)(2,1)} %bitcast.63, bf16[]{:T(256)} %broadcast.138), dimensions={1}, to_apply=%bitcast.41.reduce_sub_computation | reduce | bytes 196610
  113.9 7.5 %reshape.135 = bf16[16,2,1536]{2,1,0:T(2,128)(2,1)} reshape(bf16[16384,3]{1,0:T(8,128)(2,1)} %reduce) | data formatting | bytes 196608
  121.4 7.4 %all-to-all-start.1 = ((bf16[16,2,1536]{2,1,0:T(2,128)(2,1)}), bf16[16,2,1536]{2,1,0:T(2,128)(2,1)S(1)}, u32[]{:S(2)}, u32[]{:S(2)}) async-start(bf16[16,2,1536]{2,1,0:T(2,128)(2,1)} %reshape.135), calls=%async_computation.1 | async-start | bytes 196608 | tf_op jit(solution)/shard_map/all_to_all | solution.py:32
  128.9 2.0 gather_fusion
  130.9 22.4 %all-gather.3 = bf16[16,8192]{1,0:T(8,128)(2,1)S(1)} all-gather(bf16[16,512]{1,0:T(8,128)(2,1)S(1)} %get-tuple-element.15), channel_id=5, replica_groups=mesh['groups'=2,'tensor'=16] {'tensor'}, dimensions={1}, use_global_device_ids=true | all-gather | bytes 278528 | tf_op jit(solution)/shard_map/all_gather | solution.py:41
  153.6 18.4 %all-gather.4 = bf16[16,8192]{1,0:T(8,128)(2,1)S(1)} all-gather(bf16[16,512]{1,0:T(8,128)(2,1)S(1)} %get-tuple-element.13), channel_id=6, replica_groups=mesh['groups'=2,'tensor'=16] {'tensor'}, dimensions={1}, use_global_device_ids=true | all-gather | bytes 278528 | tf_op jit(solution)/shard_map/all_gather | solution.py:41
  172.2 8.2 %fusion.2 = bf16[16,1,1024]{2,0,1:T(8,128)(2,1)S(1)} fusion(bf16[8192,1024]{1,0:T(8,128)(2,1)} %param.21, bf16[16,8192]{1,0:T(8,128)(2,1)S(1)} %all-gather.3, f32[8192]{0:T(1024)S(1)} %copy-done.2, f32[16]{0:T(128)S(1)} %add_rsqrt_fusion.5), kind=kOutput, calls=%fused_computation.13 | convolution fusion | flops 268976128 | bytes 17104960 | tf_op jit(solution)/shard_map/dot_general | solution.py:48
  180.4 8.2 %fusion.3 = bf16[16,1,1024]{2,0,1:T(8,128)(2,1)S(1)} fusion(bf16[8192,1024]{1,0:T(8,128)(2,1)} %param.21, bf16[16,8192]{1,0:T(8,128)(2,1)S(1)} %all-gather.4, f32[16]{0:T(128)S(1)} %add_rsqrt_fusion.3, f32[8192]{0:T(1024)S(1)} %copy-done.2), kind=kOutput, calls=%fused_computation.14 | convolution fusion | flops 268976128 | bytes 17104960 | tf_op jit(solution)/shard_map/dot_general | solution.py:48
  188.7 19.6 %all-gather.5 = bf16[16,8192]{1,0:T(8,128)(2,1)S(1)} all-gather(bf16[16,512]{1,0:T(8,128)(2,1)S(1)} %get-tuple-element.14), channel_id=7, replica_groups=mesh['groups'=2,'tensor'=16] {'tensor'}, dimensions={1}, use_global_device_ids=true | all-gather | bytes 278528 | tf_op jit(solution)/shard_map/all_gather | solution.py:41
  208.5 2.3 fusion.4
  211.7 12.6 %copy.57 = bf16[1,16,16384]{1,0,2:T(2,128)(2,1)} copy(bf16[1,16,16384]{2,1,0:T(8,128)(2,1)S(1)} %copy-done.6) | data formatting | bytes 1048576 | tf_op args[15]
  224.3 90.8 %reduce.1 = bf16[16384,16]{1,0:T(8,128)(2,1)} reduce(bf16[16384,1,16]{2,1,0:T(2,128)(2,1)} %bitcast.64, bf16[]{:T(256)} %broadcast.138), dimensions={1}, to_apply=%bitcast.43.reduce_sub_computation | reduce | bytes 1048578
  315.1 6.5 %reshape.137 = bf16[16,2,8192]{2,1,0:T(2,128)(2,1)} reshape(bf16[16384,16]{1,0:T(8,128)(2,1)} %reduce.1) | data formatting | bytes 1048576
  321.6 4.3 all-to-all-start
  325.9 11.9 %all-reduce.3.cloned.1.call-start = ((), (), s32[]{:S(2)}) async-start(), calls=%async_computation.6 | async-start | bytes 245760 | tf_op jit(solution)/shard_map/psum | solution.py:54
  337.8 11.1 %reshape.136 = bf16[16384,1,3]{2,1,0:T(2,128)(2,1)} reshape(bf16[16,2,1536]{2,1,0:T(2,128)(2,1)S(1)} %all-to-all-done.1) | data formatting | bytes 196608
  349.0 15.4 %copy.61 = bf16[1,3,16384]{2,1,0:T(4,128)(2,1)S(1)} copy(bf16[1,3,16384]{1,0,2:T(2,128)(2,1)} %bitcast.65) | data formatting | bytes 196608 | tf_op jit(solution)/shard_map/all_to_all | solution.py:32
  365.3 1.9 multiply_reduce_fusion.5
  367.3 1.0 fusion.46
  368.3 1.0 fusion.48
  369.3 1.0 fusion.50
  370.5 1.5 exponential_negate_fusion
  371.9 87.2 %all-reduce.3.cloned.1.call-done = (f32[16,544]{1,0:T(8,128)}, f32[16,544]{1,0:T(8,128)}, f32[16,544]{1,0:T(8,128)}) async-done(((f32[16,544]{1,0:T(8,128)}, f32[16,544]{1,0:T(8,128)}, f32[16,544]{1,0:T(8,128)}), (f32[16,544]{1,0:T(8,128)}, f32[16,544]{1,0:T(8,128)}, f32[16,544]{1,0:T(8,128)})) %all-reduce.3.cloned.1.call-update) | async-done | bytes 104464 | tf_op jit(solution)/shard_map/psum | solution.py:54
  459.1 0.9 multiply_reduce_fusion.8
  460.0 0.9 fusion.64
  460.8 0.9 multiply_reduce_fusion.6
  462.6 1.1 compare_select_fusion.2
  463.7 1.1 compare_select_fusion.1
  464.8 1.8 fusion.62
  466.5 11.6 %reshape.138 = bf16[16384,1,16]{2,1,0:T(2,128)(2,1)} reshape(bf16[16,2,8192]{2,1,0:T(2,128)(2,1)} %all-to-all-done) | data formatting | bytes 1048576
  478.2 14.9 %copy.58 = bf16[1,16,16384]{2,1,0:T(8,128)(2,1)S(1)} copy(bf16[1,16,16384]{1,0,2:T(2,128)(2,1)} %bitcast.66) | data formatting | bytes 1048576 | tf_op jit(solution)/shard_map/all_to_all | solution.py:31
  493.7 3.1 multiply_reduce_fusion.1
  496.8 8.3 %fusion.43 = bf16[1,16,1024]{2,1,0:T(8,128)(2,1)S(1)} fusion(bf16[8192,1024]{1,0:T(8,128)(2,1)} %param.22, bf16[16,8192]{1,0:T(8,128)(2,1)S(1)} %all-gather.3, f32[8192]{0:T(1024)S(1)} %copy-done.2, f32[16]{0:T(128)S(1)} %add_rsqrt_fusion.5, f32[16,1024]{1,0:T(8,128)S(1)} %get-tuple-element.5, f32[1024]{0:T(1024)S(1)} %copy-done.10, ...), kind=kOutput, calls=%fused_computation.67 | convolution fusion | flops 269172736 | bytes 17244224 | tf_op jit(solution)/shard_map/dot_general | solution.py:49
  505.1 8.9 %fusion.35 = bf16[1,16,1024]{2,1,0:T(8,128)(2,1)} fusion(bf16[8192,1024]{1,0:T(8,128)(2,1)} %param.22, bf16[16,8192]{1,0:T(8,128)(2,1)S(1)} %all-gather.4, f32[16]{0:T(128)S(1)} %add_rsqrt_fusion.3, f32[8192]{0:T(1024)S(1)} %copy-done.2, f32[16,1024]{1,0:T(8,128)S(1)} %get-tuple-element.3, f32[1024]{0:T(1024)S(1)} %copy-done.10, ...), kind=kOutput, calls=%fused_computation.65 | convolution fusion | flops 269172736 | bytes 17244224 | tf_op jit(solution)/shard_map/dot_general | solution.py:49
  514.0 3.0 fusion.27
  517.1 1.2 slice-done.11
  518.4 5.0 fusion
  523.4 1.1 fusion.15
  525.2 2.4 scatter_fusion.1
  527.7 6.8 %all-to-all-start.3 = ((bf16[16,3,1024]{2,1,0:T(4,128)(2,1)}), bf16[16,3,1024]{2,1,0:T(4,128)(2,1)S(1)}, u32[]{:S(2)}, u32[]{:S(2)}) async-start(bf16[16,3,1024]{2,1,0:T(4,128)(2,1)} %scatter_fusion.1), calls=%async_computation.4 | async-start | bytes 262144 | tf_op jit(solution)/shard_map/all_to_all | solution.py:85
  534.5 0.9 broadcast_in_dim.16
  535.3 2.6 scatter_fusion
  537.9 4.5 all-to-all-done.3
  542.4 3.6 all-to-all-start.2
  546.0 16.5 %all-to-all-done.2 = bf16[16,16,1024]{2,1,0:T(8,128)(2,1)S(1)} async-done(((bf16[16,16,1024]{2,1,0:T(8,128)(2,1)}), bf16[16,16,1024]{2,1,0:T(8,128)(2,1)S(1)}, u32[]{:S(2)}, u32[]{:S(2)}) %all-to-all-start.2) | async-done | bytes 524320 | tf_op jit(solution)/shard_map/all_to_all | solution.py:84
  563.3 23.0 %reduce-scatter.2.cloned.1.call-done = f32[3,16,512]{2,1,0:T(8,128)} async-done(((f32[3,16,8192]{2,1,0:T(8,128)}), f32[3,16,512]{2,1,0:T(8,128)}) %reduce-scatter.2.cloned.1.call-update) | async-done | bytes 98320 | tf_op jit(solution)/shard_map/reduce_scatter | solution.py:78
  586.3 1.5 fusion.21
  (93 shorter events, 6.9 us)
Async XLA Ops:
  7.2 360.1 %copy-start = (bf16[1024,544]{0,1:T(8,128)(2,1)S(1)}, bf16[1024,544]{0,1:T(8,128)(2,1)}, u32[]{:S(2)}) copy-start(bf16[1024,544]{0,1:T(8,128)(2,1)} %param.25) | copy-start | bytes 3342340
  7.2 121.6 %copy-start.15 = (s32[3,16]{1,0:T(4,128)S(1)}, s32[3,16]{1,0:T(4,128)}, u32[]{:S(2)}) copy-start(s32[3,16]{1,0:T(4,128)} %param.17) | copy-start | bytes 580
  7.2 165.0 %copy-start.2 = (f32[8192]{0:T(1024)S(1)}, f32[8192]{0:T(1024)}, u32[]{:S(2)}) copy-start(f32[8192]{0:T(1024)} %param.20) | copy-start | bytes 98308
  121.4 200.3 %all-to-all-start.1 = ((bf16[16,2,1536]{2,1,0:T(2,128)(2,1)}), bf16[16,2,1536]{2,1,0:T(2,128)(2,1)S(1)}, u32[]{:S(2)}, u32[]{:S(2)}) async-start(bf16[16,2,1536]{2,1,0:T(2,128)(2,1)} %reshape.135), calls=%async_computation.1 | async-start | bytes 196608 | tf_op jit(solution)/shard_map/all_to_all | solution.py:32
  130.9 49.5 %copy-start.7 = (bf16[48,512]{1,0:T(8,128)(2,1)}, bf16[48,512]{1,0:T(8,128)(2,1)S(1)}, u32[]{:S(2)}) copy-start(bf16[48,512]{1,0:T(8,128)(2,1)S(1)} %gather_fusion) | copy-start | bytes 147460
  172.2 36.3 %slice-start = ((s8[16777216]{0:T(1024)(128)(4,1)}), s8[4194304]{0:T(1024)(128)(4,1)S(1)}, s32[]{:S(2)}) async-start(s8[16777216]{0:T(1024)(128)(4,1)} %bitcast.59), calls=%async_computation.7 | async-start | bytes 8388608
  172.2 36.3 %slice-start.1 = ((s8[16777216]{0:T(1024)(128)(4,1)}), s8[4194304]{0:T(1024)(128)(4,1)S(1)}, s32[]{:S(2)}) async-start(s8[16777216]{0:T(1024)(128)(4,1)} %bitcast.59), calls=%async_computation.8 | async-start | bytes 8388608
  180.4 28.1 %slice-start.2 = ((s8[16777216]{0:T(1024)(128)(4,1)}), s8[4194304]{0:T(1024)(128)(4,1)S(1)}, s32[]{:S(2)}) async-start(s8[16777216]{0:T(1024)(128)(4,1)} %bitcast.59), calls=%async_computation.9 | async-start | bytes 8388608
  180.4 28.1 %slice-start.3 = ((s8[16777216]{0:T(1024)(128)(4,1)}), s8[4194304]{0:T(1024)(128)(4,1)S(1)}, s32[]{:S(2)}) async-start(s8[16777216]{0:T(1024)(128)(4,1)} %bitcast.59), calls=%async_computation.10 | async-start | bytes 8388608
  188.7 22.2 %copy-start.16 = (s32[16,2]{0,1:T(2,128)S(1)}, s32[16,2]{0,1:T(2,128)}, u32[]{:S(2)}) copy-start(s32[16,2]{0,1:T(2,128)} %param.18) | copy-start | bytes 388
  188.7 23.0 %copy-start.6 = (bf16[1,16,16384]{2,1,0:T(8,128)(2,1)S(1)}, bf16[1,16,16384]{2,1,0:T(8,128)(2,1)}, u32[]{:S(2)}) copy-start(bf16[1,16,16384]{2,1,0:T(8,128)(2,1)} %param.32) | copy-start | bytes 1572868
  210.9 138.1 %copy-start.13 = (s32[16]{0:T(128)}, s32[16]{0:T(128)S(1)}, u32[]{:S(2)}) copy-start(s32[16]{0:T(128)S(1)} %fusion.58) | copy-start | bytes 196
  210.9 154.2 %copy-start.5 = (bf16[16,1,1024]{2,1,0:T(2,128)(2,1)}, bf16[16,1,1024]{2,1,0:T(2,128)(2,1)S(1)}, u32[]{:S(2)}) copy-start(bf16[16,1,1024]{2,1,0:T(2,128)(2,1)S(1)} %copy.63) | copy-start | bytes 98308
  211.0 154.3 %copy-start.4 = (bf16[16,1,1024]{2,1,0:T(2,128)(2,1)}, bf16[16,1,1024]{2,1,0:T(2,128)(2,1)S(1)}, u32[]{:S(2)}) copy-start(bf16[16,1,1024]{2,1,0:T(2,128)(2,1)S(1)} %copy.65) | copy-start | bytes 98308
  224.3 141.0 %copy-start.12 = (f32[4,1024]{1,0:T(4,128)S(1)}, f32[4,1024]{1,0:T(4,128)}, u32[]{:S(2)}) copy-start(f32[4,1024]{1,0:T(4,128)} %param.23) | copy-start | bytes 49156
  224.3 143.0 %copy-start.8 = (f32[1024]{0:T(1024)S(1)}, f32[1024]{0:T(1024)}, u32[]{:S(2)}) copy-start(f32[1024]{0:T(1024)} %param.24) | copy-start | bytes 12292
  315.1 147.5 %copy-start.1 = (bf16[512,1024]{1,0:T(8,128)(2,1)S(1)}, bf16[512,1024]{1,0:T(8,128)(2,1)}, u32[]{:S(2)}) copy-start(bf16[512,1024]{1,0:T(8,128)(2,1)} %param.27) | copy-start | bytes 3145732
  315.1 147.5 %copy-start.9 = (f32[1024]{0:T(1024)S(1)}, f32[1024]{0:T(1024)}, u32[]{:S(2)}) copy-start(f32[1024]{0:T(1024)} %param.28) | copy-start | bytes 12292
  315.1 147.5 %copy-start.11 = (f32[512]{0:T(512)S(1)}, f32[512]{0:T(512)}, u32[]{:S(2)}) copy-start(f32[512]{0:T(512)} %param.26) | copy-start | bytes 6148
  321.6 144.9 %all-to-all-start = ((bf16[16,2,8192]{2,1,0:T(2,128)(2,1)}), bf16[16,2,8192]{2,1,0:T(2,128)(2,1)}, u32[]{:S(2)}, u32[]{:S(2)}) async-start(bf16[16,2,8192]{2,1,0:T(2,128)(2,1)} %reshape.137), calls=%async_computation | async-start | bytes 1048576 | tf_op jit(solution)/shard_map/all_to_all | solution.py:31
  325.9 133.2 %all-reduce.3.cloned.1.call-start = ((), (), s32[]{:S(2)}) async-start(), calls=%async_computation.6 | async-start | bytes 245760 | tf_op jit(solution)/shard_map/psum | solution.py:54
  364.3 132.5 %copy-start.10 = (f32[1024]{0:T(1024)S(1)}, f32[1024]{0:T(1024)}, u32[]{:S(2)}) copy-start(f32[1024]{0:T(1024)} %param.30) | copy-start | bytes 12292
  370.4 215.9 %reduce-scatter.2.cloned.1.call-start = ((), (), s32[]{:S(2)}) async-start(), calls=%async_computation.5 | async-start | bytes 1671168 | tf_op jit(solution)/shard_map/reduce_scatter | solution.py:78
  496.8 17.2 %slice-start.4 = ((s8[16777216]{0:T(1024)(128)(4,1)}), s8[4194304]{0:T(1024)(128)(4,1)S(1)}, s32[]{:S(2)}) async-start(s8[16777216]{0:T(1024)(128)(4,1)} %bitcast.61), calls=%async_computation.11 | async-start | bytes 8388608
  496.8 17.2 %slice-start.5 = ((s8[16777216]{0:T(1024)(128)(4,1)}), s8[4194304]{0:T(1024)(128)(4,1)S(1)}, s32[]{:S(2)}) async-start(s8[16777216]{0:T(1024)(128)(4,1)} %bitcast.61), calls=%async_computation.12 | async-start | bytes 8388608
  505.1 8.9 %slice-start.6 = ((s8[16777216]{0:T(1024)(128)(4,1)}), s8[4194304]{0:T(1024)(128)(4,1)S(1)}, s32[]{:S(2)}) async-start(s8[16777216]{0:T(1024)(128)(4,1)} %bitcast.61), calls=%async_computation.13 | async-start | bytes 8388608
  505.1 8.9 %slice-start.7 = ((s8[16777216]{0:T(1024)(128)(4,1)}), s8[4194304]{0:T(1024)(128)(4,1)S(1)}, s32[]{:S(2)}) async-start(s8[16777216]{0:T(1024)(128)(4,1)} %bitcast.61), calls=%async_computation.14 | async-start | bytes 8388608
  505.1 11.9 %slice-start.8 = ((s8[16777216]{0:T(1024)(128)(4,1)}), s8[4194304]{0:T(1024)(128)(4,1)S(1)}, s32[]{:S(2)}) async-start(s8[16777216]{0:T(1024)(128)(4,1)} %bitcast.67), calls=%async_computation.15 | async-start | bytes 8388608
  505.1 11.9 %slice-start.9 = ((s8[16777216]{0:T(1024)(128)(4,1)}), s8[4194304]{0:T(1024)(128)(4,1)S(1)}, s32[]{:S(2)}) async-start(s8[16777216]{0:T(1024)(128)(4,1)} %bitcast.67), calls=%async_computation.16 | async-start | bytes 8388608
  514.0 3.1 slice-start.10
  514.0 4.3 slice-start.11
  518.4 6.9 %copy-start.14 = (s32[16]{0:T(128)S(1)}, s32[16]{0:T(128)}, u32[]{:S(2)}) copy-start(s32[16]{0:T(128)} %copy-done.13) | copy-start | bytes 196
  518.4 17.0 %copy-start.3 = (bf16[16,16,1024]{2,1,0:T(8,128)(2,1)S(1)}, bf16[16,16,1024]{2,1,0:T(8,128)(2,1)}, u32[]{:S(2)}) copy-start(bf16[16,16,1024]{2,1,0:T(8,128)(2,1)} %get-tuple-element.12) | copy-start | bytes 1572868
  527.7 14.7 %all-to-all-start.3 = ((bf16[16,3,1024]{2,1,0:T(4,128)(2,1)}), bf16[16,3,1024]{2,1,0:T(4,128)(2,1)S(1)}, u32[]{:S(2)}, u32[]{:S(2)}) async-start(bf16[16,3,1024]{2,1,0:T(4,128)(2,1)} %scatter_fusion.1), calls=%async_computation.4 | async-start | bytes 262144 | tf_op jit(solution)/shard_map/all_to_all | solution.py:85
  542.4 20.1 %all-to-all-start.2 = ((bf16[16,16,1024]{2,1,0:T(8,128)(2,1)}), bf16[16,16,1024]{2,1,0:T(8,128)(2,1)S(1)}, u32[]{:S(2)}, u32[]{:S(2)}) async-start(bf16[16,16,1024]{2,1,0:T(8,128)(2,1)} %scatter_fusion), calls=%async_computation.3 | async-start | bytes 1048576 | tf_op jit(solution)/shard_map/all_to_all | solution.py:84
Sparse Core Ops, SparseCore 0:
  370.5 88.5 all-reduce.2
  523.5 62.7 reduce-scatter.1
where the time goes:
time: 600 us; the launch traced here: 596 us
  other arithmetic  193 us (32%)
  waiting for transfers between devices  131 us (22%)
  local copies, waits for them, and re-layouts  111 us (18%)
  blocking collectives  60.4 us (10%)
  matrix products  50.9 us (8%)
  starting transfers between devices  34 us (6%)
  between operations  14.7 us (2%)
    unnamed x5, other arithmetic  182 us
    psum x1, waiting for transfers between devices, body(): projected = lax.psum(partial_proj, 'tensor')  87.2 us
    unnamed x66, local copies, waits for them, and re-layouts  67.5 us
    all_gather x3, blocking collectives, body(): lax.all_gather(local_rows[position], 'tensor', axis=1, tiled=True)  60.4 us
    reduce_scatter x1, waiting for transfers between devices, body(): lax.psum_scatter(partial_all, 'tensor', scatter_dimension=2, tiled=True)  23 us
    dot_general x3, matrix products, body(): z_inner = jnp.dot(normed, z_weight, preferred_element_type=jnp.float32)  20.1 us
    dot_general x3, matrix products, body(): jnp.dot(normed, x_weight, preferred_element_type=jnp.float32)  18.8 us
    all_to_all x1, waiting for transfers between devices, body(): lax.all_to_all(state_back, 'tensor', split_axis=0, concat_axis=2, tiled=T...  16.5 us
  transfers between devices with their start and end apart: 6, of which 4 were waited for; matrix products, arithmetic and copies ran while one was open for 31% of the time, Pallas kernels for 0%

commit v1 on v0

v1 whole, which is shorter than its diff:
```python
import functools

import jax
import jax.numpy as jnp
from jax import lax
from jax.experimental import pallas as pl
from jax.experimental.pallas import tpu as pltpu
from jax.sharding import PartitionSpec as P

LANES = 128
F32 = jnp.float32
BF16 = jnp.bfloat16


def sigmoid(v):
    return 1.0 / (1.0 + jnp.exp(-v))


def kernel(
    n, steps, slots, rank, states,
    rows_ref, gain_ref, conv_w_ref, conv_b_ref, dgain_ref, dbias_ref, lograte_ref, skip_ref,
    xw_hbm, zw_hbm, proj_hbm, dw_hbm, ow_hbm, ssm_hbm, conv_hbm,
    hid_ref, ssm_out, conv_out,
    xw, zw, ow, pw, dw,
    gath, accx, accz, ssq, state_in, state_fin, conv_in, conv_fin, win, act, delta, ysum,
    pf, part, part_in, red_out, proj_all, proj_f, mats, gated,
    send_a, recv_a, send_b, recv_b, send_c, recv_c,
    xw_sem, zw_sem, ow_sem, misc_sem,
    g_recv, g_s1, g_s2, g_s3,
    st_recv, st_send, cv_recv, cv_send,
    p_recv, p_send, q_recv, q_send,
    a_recv, a_send, b_recv, b_send, c_recv, c_send,
    so_recv, so_send, co_recv, co_send,
):
    me = lax.axis_index("tensor")
    bits = n.bit_length() - 1

    def xor(a, b):
        if isinstance(a, int) and isinstance(b, int):
            return a ^ b
        out = 0
        for k in range(bits):
            out = out + ((a // (1 << k)) % 2 + (b // (1 << k)) % 2) % 2 * (1 << k)
        return out

    rows = rows_ref.shape[0]
    per = rows // steps
    dl = rows_ref.shape[1]
    cl = accx.shape[1]
    d_model = n * dl
    q = n // 4

    def order(i):
        return (i % (n // 2)) // 2 * 4 + i // (n // 2) * 2 + i % 2

    def out_order(i):
        return jnp.where(
            i < n // 2, 2 * i + 1,
            jnp.where(i < n // 2 + q, 4 * (i - n // 2) + 2, (4 * (i - n // 2 - q) + 4) % n),
        )

    def cols(owner, width):
        return pl.ds(pl.multiple_of(owner * width, width), width)

    def x_load(i):
        src = xw_hbm.at[cols(xor(me, order(i)), dl), :]
        return pltpu.make_async_copy(src, xw.at[i], xw_sem.at[i])

    def z_load(i):
        src = zw_hbm.at[cols(xor(me, order(i)), dl), :]
        return pltpu.make_async_copy(src, zw.at[i], zw_sem.at[i])

    def o_load(i):
        if dl % LANES == 0:
            src = ow_hbm.at[:, cols(xor(me, out_order(i)), dl)]
        else:
            src = ow_hbm.at[xor(me, out_order(i))]
        return pltpu.make_async_copy(src, ow.at[i], ow_sem.at[i])

    p_load = pltpu.make_async_copy(proj_hbm, pw, misc_sem.at[0])
    d_load = pltpu.make_async_copy(dw_hbm, dw, misc_sem.at[1])
    own_state = pltpu.make_async_copy(ssm_hbm.at[:, :, cols(me, cl)], state_in.at[me], misc_sem.at[2])
    own_conv = pltpu.make_async_copy(conv_hbm.at[:, :, cols(me, cl)], conv_in.at[me], misc_sem.at[3])

    def remote(src, dst, ssem, rsem, peer):
        return pltpu.make_async_remote_copy(
            src_ref=src, dst_ref=dst, send_sem=ssem, recv_sem=rsem,
            device_id={"tensor": peer}, device_id_type=pl.DeviceIdType.MESH,
        )

    def to_core(j):
        return remote(gath.at[j], gath.at[j + 1], g_s1.at[j // 2], g_recv.at[j + 1], xor(me, 1))

    def to_side(j):
        return remote(gath.at[j], gath.at[j + 2], g_s2.at[j // 4], g_recv.at[j + 2], xor(me, 2))

    def to_far(k):
        return remote(gath.at[0], gath.at[4 * k], g_s3.at[k], g_recv.at[4 * k], xor(me, 4 * k))

    def got(j):
        return remote(gath.at[0], gath.at[j], g_s3.at[0], g_recv.at[j], xor(me, 1)).wait_recv()

    def state_copy(j, at):
        return remote(ssm_hbm.at[:, :, cols(xor(me, j), cl)], state_in.at[at], st_send.at[j], st_recv.at[j], xor(me, j))

    def conv_copy(j, at):
        return remote(conv_hbm.at[:, :, cols(xor(me, j), cl)], conv_in.at[at], cv_send.at[j], cv_recv.at[j], xor(me, j))

    def loop(lo, hi):
        def wrap(f):
            lax.fori_loop(lo, hi, lambda i, c: (f(i), c)[1], 0)
        return wrap

    @loop(0, min(4, n))
    def _(i):
        x_load(i).start()
        z_load(i).start()

    barrier = pltpu.get_barrier_semaphore()

    @loop(1, n)
    def _(j):
        pl.semaphore_signal(barrier, inc=1, device_id={"tensor": xor(me, j)}, device_id_type=pl.DeviceIdType.MESH)

    gath[0] = rows_ref[...]

    @loop(min(4, n), n)
    def _(i):
        x_load(i).start()
        z_load(i).start()

    p_load.start()
    d_load.start()
    own_state.start()
    own_conv.start()
    pl.semaphore_wait(barrier, n - 1)

    @loop(1, q)
    def _(k):
        to_far(k).start()

    to_side(0).start()
    to_core(0).start()

    accx[...] = jnp.zeros_like(accx)
    accz[...] = jnp.zeros_like(accz)
    ssq[...] = jnp.zeros_like(ssq)
    pf[...] = jnp.zeros_like(pf)

    @loop(0, n)
    def _(i):
        @pl.when(i >= 1)
        def _():
            conv_copy(i, me).start()
            state_copy(i, me).start()

        @pl.when((i % 2 == 0) & (i + 2 < n))
        def _():
            j = order(i + 2)
            got(j)
            to_core(j).start()

            @pl.when(j % 4 == 0)
            def _():
                to_side(j).start()

        j = order(i)

        @pl.when(i % 2 == 1)
        def _():
            got(j)

        e = gath[j].astype(F32)
        ssq[...] += jnp.sum(e * e, axis=1, keepdims=True)
        a = (e * gain_ref[xor(me, j)]).astype(BF16)
        x_load(i).wait()
        accx[...] += jnp.dot(a, xw[i], preferred_element_type=F32)
        z_load(i).wait()
        accz[...] += jnp.dot(a, zw[i], preferred_element_type=F32)

    @loop(0, n)
    def _(i):
        o_load(i).start()

    own_conv.wait()

    @loop(1, n)
    def _(j):
        conv_copy(j, xor(me, j)).wait_recv()

    @loop(0, n)
    def _(r):
        for s in range(slots):
            w = conv_in[r, s].astype(F32)
            for k in range(w.shape[0]):
                win[pl.ds(k * per + r * slots + s, 1), :] = w[k : k + 1]

    scale = lax.rsqrt(ssq[...] / d_model + 1e-06)
    taps = conv_w_ref.shape[0]
    win[pl.ds((taps - 1) * per, rows), :] = (accx[...] * scale).astype(BF16).astype(F32)
    zv = accz[...] * scale
    accz[...] = zv * sigmoid(zv)
    for t in range(steps):
        pre = conv_b_ref[...]
        for k in range(taps):
            pre = pre + win[pl.ds((t + k) * per, per), :] * conv_w_ref[k : k + 1]
        act[pl.ds(t * per, per), :] = pre * sigmoid(pre)

    p_load.wait()
    width = proj_hbm.shape[1]
    pf[:, :width] = jnp.dot(act[...].astype(BF16), pw[...], preferred_element_type=F32)
    blocks = pf.shape[1] // LANES
    tiles = part.shape[1]
    used = rows // 16 * blocks
    for k in range(used, n * tiles):
        part[k // tiles, k % tiles] = jnp.zeros((16, LANES), BF16)
    for k in range(used):
        g, b = divmod(k, blocks)
        part[k // tiles, k % tiles] = pf[16 * g : 16 * g + 16, LANES * b : LANES * b + LANES].astype(BF16)

    def sum_copy(j):
        return remote(part.at[xor(me, j)], part_in.at[j], p_send.at[j], p_recv.at[j], xor(me, j))

    def share_copy(j, at):
        return remote(red_out, proj_all.at[at], q_send.at[j], q_recv.at[j], xor(me, j))

    @loop(1, n)
    def _(j):
        sum_copy(n - j).start()

    part_in[0] = part[me]

    @loop(1, n)
    def _(j):
        sum_copy(j).wait_recv()

    red = jnp.sum(part_in[...].astype(F32), axis=0).astype(BF16)
    red_out[...] = red
    proj_all[me] = red

    @loop(1, n)
    def _(j):
        share_copy(n - j, me).start()

    @loop(1, n)
    def _(j):
        share_copy(j, xor(me, j)).wait_recv()

    for k in range(used):
        g, b = divmod(k, blocks)
        proj_f[16 * g : 16 * g + 16, LANES * b : LANES * b + LANES] = proj_all[k // tiles, k % tiles].astype(F32)

    low = proj_f[:, :rank]
    mats[...] = proj_f[:, rank : rank + LANES]
    norm = (low * lax.rsqrt(jnp.mean(low * low, axis=1, keepdims=True) + 1e-06) * dgain_ref[...]).astype(BF16)
    d_load.wait()
    pre = jnp.dot(norm, dw[...], preferred_element_type=F32) + dbias_ref[...]
    delta[...] = jnp.maximum(pre, 0.0) + jnp.log1p(jnp.exp(-jnp.abs(pre)))

    own_state.wait()
    rates = -jnp.exp(lograte_ref[...])

    def state_back(j, at):
        return remote(state_fin.at[xor(me, j)], ssm_out.at[:, :, cols(at, cl)], so_send.at[j], so_recv.at[j], xor(me, j))

    def conv_back(j, at):
        return remote(conv_fin.at[xor(me, j)], conv_out.at[:, :, cols(at, cl)], co_send.at[j], co_recv.at[j], xor(me, j))

    own_state_back = pltpu.make_async_copy(state_fin.at[me], ssm_out.at[:, :, cols(me, cl)], misc_sem.at[2])
    own_conv_back = pltpu.make_async_copy(conv_fin.at[me], conv_out.at[:, :, cols(me, cl)], misc_sem.at[3])
    lane = lax.broadcasted_iota(jnp.int32, (2 * states, LANES), 1)
    diag = lane == lax.broadcasted_iota(jnp.int32, (2 * states, LANES), 0)

    @loop(0, n)
    def _(i):
        j = n - 1 - i
        owner = xor(me, j)

        @pl.when(j > 0)
        def _():
            state_copy(j, owner).wait_recv()

        for s in range(slots):
            r = owner * slots + s
            h = state_in[owner, s].astype(F32)
            kept = []
            for t in range(steps):
                at = pl.ds(t * per + r, 1)
                both = jnp.sum(jnp.where(diag, mats[at, :], 0.0), axis=1, keepdims=True)
                dt = delta[at, :]
                h = h * jnp.exp(dt * rates) + (dt * act[at, :]) * both[:states]
                ysum[at, :] = jnp.sum(h * both[states:], axis=0, keepdims=True)
            state_fin[owner, s] = h.astype(BF16)
            kept = [win[pl.ds((steps + k) * per + r, 1), :] for k in range(taps - 1)]
            conv_fin[owner, s] = jnp.concatenate(kept, axis=0).astype(BF16)

        @pl.when(j > 0)
        def _():
            state_back(j, me).start()
            conv_back(j, me).start()

    own_state_back.start()
    own_conv_back.start()
    gated[...] = ((ysum[...] + skip_ref[...] * act[...]) * accz[...]).astype(BF16)

    def a_copy(k):
        return remote(send_a.at[k], recv_a.at[k], a_send.at[k], a_recv.at[k], xor(me, 1))

    def b_copy(k):
        return remote(send_b.at[k], recv_b.at[k], b_send.at[k], b_recv.at[k], xor(me, 2))

    def c_copy(k):
        return remote(send_c.at[k], recv_c.at[k], c_send.at[k], c_recv.at[k], xor(me, 4 * k))

    def product(i):
        o_load(i).wait()
        return jnp.dot(gated[...], ow[i], preferred_element_type=F32)

    @loop(0, n // 2)
    def _(i):
        send_a[i] = product(i).astype(BF16)
        a_copy(i).start()

    @loop(0, q)
    def _(k):
        total = product(n // 2 + k)
        a_copy(2 * k + 1).wait_recv()
        send_b[k] = (total + recv_a[2 * k + 1].astype(F32)).astype(BF16)
        b_copy(k).start()

    @loop(1, q)
    def _(k):
        total = product(n // 2 + q + k - 1)
        a_copy(2 * k).wait_recv()
        b_copy(k).wait_recv()
        send_c[k] = (total + recv_a[2 * k].astype(F32) + recv_b[k].astype(F32)).astype(BF16)
        c_copy(k).start()

    total = product(n - 1) + rows_ref[...].astype(F32)
    a_copy(0).wait_recv()
    b_copy(0).wait_recv()
    accum = total + recv_a[0].astype(F32) + recv_b[0].astype(F32)
    recv_c[0] = jnp.zeros((rows, dl), BF16)

    @loop(1, q)
    def _(k):
        c_copy(k).wait_recv()

    hid_ref[...] = (accum + jnp.sum(recv_c[...].astype(F32), axis=0)).astype(BF16)

    own_state_back.wait()
    own_conv_back.wait()

    @loop(1, n)
    def _(j):
        state_back(j, xor(me, j)).wait_recv()
        conv_back(j, xor(me, j)).wait_recv()
        state_back(j, me).wait_send()
        conv_back(j, me).wait_send()
        state_copy(j, me).wait_send()
        conv_copy(j, me).wait_send()
        sum_copy(j).wait_send()
        share_copy(j, me).wait_send()

    @loop(1, q)
    def _(k):
        to_far(k).wait_send()
        c_copy(k).wait_send()

    @loop(0, q)
    def _(k):
        to_side(4 * k).wait_send()
        b_copy(k).wait_send()

    @loop(0, n // 2)
    def _(k):
        to_core(2 * k).wait_send()
        a_copy(k).wait_send()


def body(
    n, tokens, page_table, embedding, norm_gain, x_weight, z_weight, conv_weight, conv_bias, proj_weight,
    delta_gain, delta_weight, delta_bias, log_rates, skip_gain, out_weight, ssm_pages, conv_pages,
):
    steps, per = tokens.shape
    slots, states, _ = ssm_pages.shape
    window = conv_pages.shape[1]
    rank, cl = delta_weight.shape
    dl = embedding.shape[1]
    rows = steps * per
    q = n // 4
    page = page_table[:, 0] * slots + page_table[:, 1]
    hit = page[:, None] == jnp.arange(per, dtype=page.dtype)[None]
    paged = jnp.sum(jnp.where(hit[None], tokens[:, :, None], 0), axis=1)
    local_rows = embedding[paged.reshape(-1)]
    width = proj_weight.shape[1]
    blocks = -(-width // LANES)
    tiles = -(-(rows // 16 * blocks) // n)
    if dl % LANES == 0:
        out_w = out_weight
    else:
        out_w = out_weight.reshape(cl, n, dl).transpose(1, 0, 2)
    vm = pl.BlockSpec(memory_space=pltpu.VMEM)
    hbm = pl.BlockSpec(memory_space=pl.ANY)
    dma = pltpu.SemaphoreType.DMA
    V = pltpu.VMEM
    hid, ssm_out, conv_out = pl.pallas_call(
        functools.partial(kernel, n, steps, slots, rank, states),
        out_shape=(
            jax.ShapeDtypeStruct((rows, dl), BF16),
            jax.ShapeDtypeStruct(ssm_pages.shape, BF16),
            jax.ShapeDtypeStruct(conv_pages.shape, BF16),
        ),
        in_specs=[vm] * 8 + [hbm] * 7,
        out_specs=(vm, hbm, hbm),
        scratch_shapes=[
            V((n, dl, cl), BF16), V((n, dl, cl), BF16), V((n, cl, dl), BF16), V((cl, width), BF16), V((rank, cl), BF16),
            V((n, rows, dl), BF16), V((rows, cl), F32), V((rows, cl), F32), V((rows, 1), F32),
            V((n, slots, states, cl), BF16), V((n, slots, states, cl), BF16),
            V((n, slots, window, cl), BF16), V((n, slots, window, cl), BF16),
            V((window * per + rows, cl), F32), V((rows, cl), F32), V((rows, cl), F32), V((rows, cl), F32),
            V((rows, blocks * LANES), F32), V((n, tiles, 16, LANES), BF16), V((n, tiles, 16, LANES), BF16),
            V((tiles, 16, LANES), BF16), V((n, tiles, 16, LANES), BF16), V((rows, blocks * LANES), F32), V((rows, LANES), F32), V((rows, cl), BF16),
            V((n // 2, rows, dl), BF16), V((n // 2, rows, dl), BF16),
            V((q, rows, dl), BF16), V((q, rows, dl), BF16), V((q, rows, dl), BF16), V((q, rows, dl), BF16),
            dma((n,)), dma((n,)), dma((n,)), dma((4,)),
            dma((n,)), dma((n // 2,)), dma((q,)), dma((q,)),
        ] + [dma((n,))] * 8 + [
            dma((n // 2,)), dma((n // 2,)), dma((q,)), dma((q,)), dma((q,)), dma((q,)),
        ] + [dma((n,))] * 4,
        compiler_params=pltpu.CompilerParams(
            collective_id=0, has_side_effects=True, vmem_limit_bytes=62 * 1024 * 1024
        ),
        cost_estimate=pl.CostEstimate(flops=2 * rows * cl * dl * n * 3, bytes_accessed=6 * cl * dl * n, transcendentals=0),
    )(
        local_rows, norm_gain.reshape(n, 1, dl), conv_weight, conv_bias.reshape(1, cl), delta_gain.reshape(1, rank),
        delta_bias.reshape(1, cl), log_rates, skip_gain.reshape(1, cl),
        x_weight, z_weight, proj_weight, delta_weight, out_w, ssm_pages, conv_pages,
    )
    return hid.reshape(steps, per, dl)[:, page], ssm_out, conv_out


def solution(mesh):
    placed = (
        P(None, "groups"),
        P("groups", None),
        P(None, "tensor"),
        P(),
        P(None, "tensor"),
        P(None, "tensor"),
        P(None, "tensor"),
        P("tensor"),
        P("tensor", None),
        P(),
        P(None, "tensor"),
        P("tensor"),
        P(None, "tensor"),
        P("tensor"),
        P("tensor", None),
        P(("groups", "tensor"), None, None),
        P(("groups", "tensor"), None, None),
    )
    return jax.shard_map(
        functools.partial(body, mesh.shape["tensor"]),
        mesh=mesh,
        in_specs=placed,
        out_specs=(
            P(None, "groups", "tensor"),
            P(("groups", "tensor"), None, None),
            P(("groups", "tensor"), None, None),
        ),
        check_vma=False,
    )
```

time: 600 us -> 79.1 us (0.13)
  other arithmetic: 193 us -> 1.63 us
  waiting for transfers between devices: 131 us -> 0 us
  local copies, waits for them, and re-layouts: 111 us -> 10.7 us
  Pallas kernels: 0 us -> 65.7 us
  blocking collectives: 60.4 us -> 0 us
  matrix products: 50.9 us -> 0 us
  starting transfers between devices: 34 us -> 0 us
  between operations: 14.7 us -> 0.66 us
    unnamed x5 -> x0, other arithmetic: 182 us -> none
    psum x1 -> x0, waiting for transfers between devices: 87.2 us -> none  [body(): projected = lax.psum(partial_proj, 'tensor')]
    pallas_call x0 -> x1, Pallas kernels: none -> 65.7 us  [body(): pl.pallas_call(functools.partial(kernel, n, steps, slots, rank, states),...]
    unnamed x66 -> x4, local copies, waits for them, and re-layouts: 67.5 us -> 6.52 us
    all_gather x3 -> x0, blocking collectives: 60.4 us -> none  [body(): lax.all_gather(local_rows[position], 'tensor', axis=1, tiled=True)]
    dot_general x13 -> x0, matrix products: 50.9 us -> none  [the longest x3 20.1 us: body(): z_inner = jnp.dot(normed, z_weight, preferred_element_type=jnp.float32)]
    all_to_all x4 -> x0, local copies, waits for them, and re-layouts: 31.1 us -> none  [the longest x1 15.4 us: body(): lax.all_to_all(conv_pages, 'tensor', split_axis=2, concat_axis=0, tiled=T...]
    reduce_scatter x1 -> x0, waiting for transfers between devices: 23 us -> none  [body(): lax.psum_scatter(partial_all, 'tensor', scatter_dimension=2, tiled=True)]
  transfers between devices with their start and end apart: 6 -> 0, of which waited for: 4 -> 0; matrix products, arithmetic and copies ran while one was open for 31% -> 0% of each run, Pallas kernels for 0% -> 0%
where the time goes in v1:
time: 79.1 us; the launch traced here: 78.7 us
  Pallas kernels  65.7 us (83%)
  local copies, waits for them, and re-layouts  10.7 us (14%)
  other arithmetic  1.63 us (2%)
    pallas_call x1, Pallas kernels, body(): pl.pallas_call(functools.partial(kernel, n, steps, slots, rank, states),...  65.7 us
    unnamed x4, local copies, waits for them, and re-layouts  6.52 us
    gather x1, local copies, waits for them, and re-layouts, body(): local_rows = embedding[paged.reshape(-1)]  2.69 us

profile of v1, /device:TPU:0, one launch (start us, length us, event | category | flops | bytes accessed | tf_op | source)
XLA Modules:
  0.0 78.7 jit_solution(17762015682479326940)
XLA Ops:
  0.6 0.8 fusion.1
  1.4 0.1 iota_compare_fusion
  1.5 0.8 select_reduce_fusion
  2.2 0.1 reshape.76
  2.3 2.7 %gather_fusion = bf16[48,512]{1,0:T(8,128)(2,1)} fusion(bf16[32768,512]{1,0:T(8,128)(2,1)} %param.19, s32[1024]{0:T(1024)S(1)} %pad_clamp_fusion.1), kind=kCustom, calls=%fused_computation | custom fusion | bytes 98496 | tf_op jit(solution)/shard_map/gather | solution.py:395
  5.0 2.4 %copy.24.proj_hbm = bf16[1024,544]{1,0:T(8,128)(2,1)} copy(bf16[1024,544]{0,1:T(8,128)(2,1)} %param.25) | data formatting | bytes 2228224 | tf_op args[8]
  7.4 65.7 %shard_map.184 = (bf16[48,512]{1,0:T(8,128)(2,1)}, bf16[1,16,16384]{2,1,0:T(8,128)(2,1)}, bf16[1,3,16384]{2,1,0:T(4,128)(2,1)}) custom-call(bf16[48,512]{1,0:T(8,128)(2,1)} %gather_fusion, f32[16,1,512]{2,1,0:T(1,128)} %bitcast.15, f32[4,1024]{1,0:T(4,128)} %conv_w_ref.1, f32[1,1024]{1,0:T(1,128)} %bitcast.16, f32[1,512]{1,0:T(1,128)} %bitcast.19, ...), custom_call_target="tpu_custom_call" | custom-call | flops 2415919104 | bytes 50331648 | tf_op jit(solution)/shard_map/pallas_call | solution.py:407
  73.1 0.8 %copy.25 = bf16[3,16,512]{2,0,1:T(4,128)(2,1)S(1)} copy(bf16[3,16,512]{2,1,0:T(8,128)(2,1)} %bitcast.14) | data formatting | bytes 98304 | tf_op jit(solution)/shard_map/reshape | solution.py:440
  74.0 0.6 gather_fusion.1
  74.6 0.6 copy.26
  75.2 1.9 %copy.29 = bf16[1,16,16384]{2,1,0:T(8,128)(2,1)} copy(bf16[1,16,16384]{2,1,0:T(8,128)(2,1)} %get-tuple-element.21) | data formatting | bytes 1048576
  77.1 1.6 %copy.30 = bf16[1,3,16384]{2,1,0:T(4,128)(2,1)} copy(bf16[1,3,16384]{2,1,0:T(4,128)(2,1)} %get-tuple-element.22) | data formatting | bytes 196608
  (3 shorter events, 0.0 us)

commit v2 on v1

--- a/solution.py
+++ b/solution.py
@@ -8,6 +8,8 @@
 from jax.sharding import PartitionSpec as P
 
 LANES = 128
+PIECES = 4
+SUM_TYPE = jnp.float32
 F32 = jnp.float32
 BF16 = jnp.bfloat16
 
@@ -16,9 +18,23 @@
     return 1.0 / (1.0 + jnp.exp(-v))
 
 
+def hand_on(hid, ssm, conv, hid_to, ssm_to, conv_to, sems):
+    wide = ssm.shape[2] // PIECES
+    copies = [
+        pltpu.make_async_copy(ssm.at[:, :, k * wide : k * wide + wide], ssm_to.at[:, :, k * wide : k * wide + wide], sems.at[k])
+        for k in range(PIECES)
+    ]
+    copies.append(pltpu.make_async_copy(conv, conv_to, sems.at[PIECES]))
+    copies.append(pltpu.make_async_copy(hid, hid_to, sems.at[PIECES + 1]))
+    for copy in copies:
+        copy.start()
+    for copy in copies:
+        copy.wait()
+
+
 def kernel(
     n, steps, slots, rank, states,
-    rows_ref, gain_ref, conv_w_ref, conv_b_ref, dgain_ref, dbias_ref, lograte_ref, skip_ref,
+    pages_ref, paged_ref, rows_ref, gain_ref, conv_w_ref, conv_b_ref, dgain_ref, dbias_ref, lograte_ref, skip_ref,
     xw_hbm, zw_hbm, proj_hbm, dw_hbm, ow_hbm, ssm_hbm, conv_hbm,
     hid_ref, ssm_out, conv_out,
     xw, zw, ow, pw, dw,
@@ -34,13 +50,15 @@
 ):
     me = lax.axis_index("tensor")
     bits = n.bit_length() - 1
-
-    def xor(a, b):
-        if isinstance(a, int) and isinstance(b, int):
-            return a ^ b
-        out = 0
+    flips = [(1 - 2 * lax.rem(lax.div(me, 1 << k), 2)) * (1 << k) for k in range(bits)]
+
+    def peer_of(j):
+        out = me
         for k in range(bits):
-            out = out + ((a // (1 << k)) % 2 + (b // (1 << k)) % 2) % 2 * (1 << k)
+            if isinstance(j, int):
+                out = out + flips[k] if j >> k & 1 else out
+            else:
+                out = out + lax.rem(lax.div(j, 1 << k), 2) * flips[k]
         return out
 
     rows = rows_ref.shape[0]
@@ -51,30 +69,34 @@
     q = n // 4
 
     def order(i):
-        return (i % (n // 2)) // 2 * 4 + i // (n // 2) * 2 + i % 2
+        if isinstance(i, int):
+            return (i % (n // 2)) // 2 * 4 + i // (n // 2) * 2 + i % 2
+        return lax.div(lax.rem(i, n // 2), 2) * 4 + lax.div(i, n // 2) * 2 + lax.rem(i, 2)
 
     def out_order(i):
+        if isinstance(i, int):
+            return 2 * i + 1 if i < n // 2 else 4 * (i - n // 2) + 2 if i < n // 2 + q else (4 * (i - n // 2 - q) + 4) % n
         return jnp.where(
             i < n // 2, 2 * i + 1,
-            jnp.where(i < n // 2 + q, 4 * (i - n // 2) + 2, (4 * (i - n // 2 - q) + 4) % n),
+            jnp.where(i < n // 2 + q, 4 * (i - n // 2) + 2, lax.rem(4 * jnp.maximum(i - n // 2 - q, 0) + 4, n)),
         )
 
     def cols(owner, width):
         return pl.ds(pl.multiple_of(owner * width, width), width)
 
     def x_load(i):
-        src = xw_hbm.at[cols(xor(me, order(i)), dl), :]
+        src = xw_hbm.at[cols(peer_of(order(i)), dl), :]
         return pltpu.make_async_copy(src, xw.at[i], xw_sem.at[i])
 
     def z_load(i):
-        src = zw_hbm.at[cols(xor(me, order(i)), dl), :]
+        src = zw_hbm.at[cols(peer_of(order(i)), dl), :]
         return pltpu.make_async_copy(src, zw.at[i], zw_sem.at[i])
 
     def o_load(i):
         if dl % LANES == 0:
-            src = ow_hbm.at[:, cols(xor(me, out_order(i)), dl)]
+            src = ow_hbm.at[:, cols(peer_of(out_order(i)), dl)]
         else:
-            src = ow_hbm.at[xor(me, out_order(i))]
+            src = ow_hbm.at[peer_of(out_order(i))]
         return pltpu.make_async_copy(src, ow.at[i], ow_sem.at[i])
 
     p_load = pltpu.make_async_copy(proj_hbm, pw, misc_sem.at[0])
@@ -89,26 +111,30 @@
         )
 
     def to_core(j):
-        return remote(gath.at[j], gath.at[j + 1], g_s1.at[j // 2], g_recv.at[j + 1], xor(me, 1))
+        return remote(gath.at[j], gath.at[j + 1], g_s1.at[j // 2 if isinstance(j, int) else lax.div(j, 2)], g_recv.at[j + 1], peer_of(1))
 
     def to_side(j):
-        return remote(gath.at[j], gath.at[j + 2], g_s2.at[j // 4], g_recv.at[j + 2], xor(me, 2))
+        return remote(gath.at[j], gath.at[j + 2], g_s2.at[j // 4 if isinstance(j, int) else lax.div(j, 4)], g_recv.at[j + 2], peer_of(2))
 
     def to_far(k):
-        return remote(gath.at[0], gath.at[4 * k], g_s3.at[k], g_recv.at[4 * k], xor(me, 4 * k))
+        return remote(gath.at[0], gath.at[4 * k], g_s3.at[k], g_recv.at[4 * k], peer_of(4 * k))
 
     def got(j):
-        return remote(gath.at[0], gath.at[j], g_s3.at[0], g_recv.at[j], xor(me, 1)).wait_recv()
+        return remote(gath.at[0], gath.at[j], g_s3.at[0], g_recv.at[j], peer_of(1)).wait_recv()
 
     def state_copy(j, at):
-        return remote(ssm_hbm.at[:, :, cols(xor(me, j), cl)], state_in.at[at], st_send.at[j], st_recv.at[j], xor(me, j))
+        return remote(ssm_hbm.at[:, :, cols(peer_of(j), cl)], state_in.at[at], st_send.at[j], st_recv.at[j], peer_of(j))
 
     def conv_copy(j, at):
-        return remote(conv_hbm.at[:, :, cols(xor(me, j), cl)], conv_in.at[at], cv_send.at[j], cv_recv.at[j], xor(me, j))
-
-    def loop(lo, hi):
+        return remote(conv_hbm.at[:, :, cols(peer_of(j), cl)], conv_in.at[at], cv_send.at[j], cv_recv.at[j], peer_of(j))
+
+    def loop(lo, hi, flat=True):
         def wrap(f):
-            lax.fori_loop(lo, hi, lambda i, c: (f(i), c)[1], 0)
+            if flat and hi - lo <= 16:
+                for i in range(lo, hi):
+                    f(i)
+            else:
+                lax.fori_loop(lo, hi, lambda i, c: (f(i), c)[1], 0)
         return wrap
 
     @loop(0, min(4, n))
@@ -120,9 +146,13 @@
 
     @loop(1, n)
     def _(j):
-        pl.semaphore_signal(barrier, inc=1, device_id={"tensor": xor(me, j)}, device_id_type=pl.DeviceIdType.MESH)
-
-    gath[0] = rows_ref[...]
+        pl.semaphore_signal(barrier, inc=1, device_id={"tensor": peer_of(j)}, device_id_type=pl.DeviceIdType.MESH)
+
+    page_row = paged_ref[0:1, :] * slots + paged_ref[1:2, :]
+    spread = (lax.broadcasted_iota(jnp.int32, (per, per), 0) == page_row).astype(F32).astype(BF16)
+    for t in range(steps):
+        here = jnp.dot(spread, rows_ref[pl.ds(t * per, per), :], preferred_element_type=F32)
+        gath[0, pl.ds(t * per, per), :] = here.astype(BF16)
 
     @loop(min(4, n), n)
     def _(i):
@@ -147,48 +177,54 @@
     ssq[...] = jnp.zeros_like(ssq)
     pf[...] = jnp.zeros_like(pf)
 
-    @loop(0, n)
+    @loop(0, n, False)
     def _(i):
-        @pl.when(i >= 1)
+        @pl.when(i < n // 2)
         def _():
-            conv_copy(i, me).start()
-            state_copy(i, me).start()
-
-        @pl.when((i % 2 == 0) & (i + 2 < n))
+            @pl.when(i >= 1)
+            def _():
+                conv_copy(2 * i, me).start()
+                state_copy(2 * i, me).start()
+
+            conv_copy(2 * i + 1, me).start()
+            state_copy(2 * i + 1, me).start()
+
+        @pl.when(i >= n // 2)
+        def _():
+            o_load(2 * i - n).start()
+            o_load(2 * i - n + 1).start()
+
+        @pl.when((lax.rem(i, 2) == 0) & (i + 2 < n))
         def _():
             j = order(i + 2)
             got(j)
             to_core(j).start()
 
-            @pl.when(j % 4 == 0)
+            @pl.when(lax.rem(j, 4) == 0)
             def _():
                 to_side(j).start()
 
         j = order(i)
 
-        @pl.when(i % 2 == 1)
+        @pl.when(lax.rem(i, 2) == 1)
         def _():
             got(j)
 
         e = gath[j].astype(F32)
         ssq[...] += jnp.sum(e * e, axis=1, keepdims=True)
-        a = (e * gain_ref[xor(me, j)]).astype(BF16)
+        a = (e * gain_ref[peer_of(j)]).astype(BF16)
         x_load(i).wait()
         accx[...] += jnp.dot(a, xw[i], preferred_element_type=F32)
         z_load(i).wait()
         accz[...] += jnp.dot(a, zw[i], preferred_element_type=F32)
 
-    @loop(0, n)
-    def _(i):
-        o_load(i).start()
-
     own_conv.wait()
 
     @loop(1, n)
     def _(j):
-        conv_copy(j, xor(me, j)).wait_recv()
-
-    @loop(0, n)
+        conv_copy(j, peer_of(j)).wait_recv()
+
+    @loop(0, n, False)
     def _(r):
         for s in range(slots):
             w = conv_in[r, s].astype(F32)
@@ -207,22 +243,24 @@
         act[pl.ds(t * per, per), :] = pre * sigmoid(pre)
 
     p_load.wait()
-    width = proj_hbm.shape[1]
-    pf[:, :width] = jnp.dot(act[...].astype(BF16), pw[...], preferred_element_type=F32)
+    width = proj_hbm.shape[0]
+    pf[:, :width] = lax.dot_general(
+        act[...].astype(BF16), pw[...], (((1,), (1,)), ((), ())), preferred_element_type=F32
+    )
     blocks = pf.shape[1] // LANES
     tiles = part.shape[1]
     used = rows // 16 * blocks
     for k in range(used, n * tiles):
-        part[k // tiles, k % tiles] = jnp.zeros((16, LANES), BF16)
+        part[k // tiles, k % tiles] = jnp.zeros((16, LANES), SUM_TYPE)
     for k in range(used):
         g, b = divmod(k, blocks)
-        part[k // tiles, k % tiles] = pf[16 * g : 16 * g + 16, LANES * b : LANES * b + LANES].astype(BF16)
+        part[k // tiles, k % tiles] = pf[16 * g : 16 * g + 16, LANES * b : LANES * b + LANES].astype(SUM_TYPE)
 
     def sum_copy(j):
-        return remote(part.at[xor(me, j)], part_in.at[j], p_send.at[j], p_recv.at[j], xor(me, j))
+        return remote(part.at[peer_of(j)], part_in.at[j], p_send.at[j], p_recv.at[j], peer_of(j))
 
     def share_copy(j, at):
-        return remote(red_out, proj_all.at[at], q_send.at[j], q_recv.at[j], xor(me, j))
+        return remote(red_out, proj_all.at[at], q_send.at[j], q_recv.at[j], peer_of(j))
 
     @loop(1, n)
     def _(j):
@@ -234,7 +272,7 @@
     def _(j):
         sum_copy(j).wait_recv()
 
-    red = jnp.sum(part_in[...].astype(F32), axis=0).astype(BF16)
+    red = jnp.sum(part_in[...].astype(F32), axis=0).astype(SUM_TYPE)
     red_out[...] = red
     proj_all[me] = red
 
@@ -244,7 +282,7 @@
 
     @loop(1, n)
     def _(j):
-        share_copy(j, xor(me, j)).wait_recv()
+        share_copy(j, peer_of(j)).wait_recv()
 
     for k in range(used):
         g, b = divmod(k, blocks)
@@ -261,20 +299,20 @@
     rates = -jnp.exp(lograte_ref[...])
 
     def state_back(j, at):
-        return remote(state_fin.at[xor(me, j)], ssm_out.at[:, :, cols(at, cl)], so_send.at[j], so_recv.at[j], xor(me, j))
+        return remote(state_fin.at[peer_of(j)], ssm_out.at[:, :, cols(at, cl)], so_send.at[j], so_recv.at[j], peer_of(j))
 
     def conv_back(j, at):
-        return remote(conv_fin.at[xor(me, j)], conv_out.at[:, :, cols(at, cl)], co_send.at[j], co_recv.at[j], xor(me, j))
+        return remote(conv_fin.at[peer_of(j)], conv_out.at[:, :, cols(at, cl)], co_send.at[j], co_recv.at[j], peer_of(j))
 
     own_state_back = pltpu.make_async_copy(state_fin.at[me], ssm_out.at[:, :, cols(me, cl)], misc_sem.at[2])
     own_conv_back = pltpu.make_async_copy(conv_fin.at[me], conv_out.at[:, :, cols(me, cl)], misc_sem.at[3])
     lane = lax.broadcasted_iota(jnp.int32, (2 * states, LANES), 1)
     diag = lane == lax.broadcasted_iota(jnp.int32, (2 * states, LANES), 0)
 
-    @loop(0, n)
+    @loop(0, n, False)
     def _(i):
         j = n - 1 - i
-        owner = xor(me, j)
+        owner = peer_of(j)
 
         @pl.when(j > 0)
         def _():
@@ -304,31 +342,31 @@
     gated[...] = ((ysum[...] + skip_ref[...] * act[...]) * accz[...]).astype(BF16)
 
     def a_copy(k):
-        return remote(send_a.at[k], recv_a.at[k], a_send.at[k], a_recv.at[k], xor(me, 1))
+        return remote(send_a.at[k], recv_a.at[k], a_send.at[k], a_recv.at[k], peer_of(1))
 
     def b_copy(k):
-        return remote(send_b.at[k], recv_b.at[k], b_send.at[k], b_recv.at[k], xor(me, 2))
+        return remote(send_b.at[k], recv_b.at[k], b_send.at[k], b_recv.at[k], peer_of(2))
 
     def c_copy(k):
-        return remote(send_c.at[k], recv_c.at[k], c_send.at[k], c_recv.at[k], xor(me, 4 * k))
+        return remote(send_c.at[k], recv_c.at[k], c_send.at[k], c_recv.at[k], peer_of(4 * k))
 
     def product(i):
         o_load(i).wait()
         return jnp.dot(gated[...], ow[i], preferred_element_type=F32)
 
-    @loop(0, n // 2)
+    @loop(0, n // 2, False)
     def _(i):
         send_a[i] = product(i).astype(BF16)
         a_copy(i).start()
 
-    @loop(0, q)
+    @loop(0, q, False)
     def _(k):
         total = product(n // 2 + k)
         a_copy(2 * k + 1).wait_recv()
         send_b[k] = (total + recv_a[2 * k + 1].astype(F32)).astype(BF16)
         b_copy(k).start()
 
-    @loop(1, q)
+    @loop(1, q, False)
     def _(k):
         total = product(n // 2 + q + k - 1)
         a_copy(2 * k).wait_recv()
@@ -336,7 +374,7 @@
         send_c[k] = (total + recv_a[2 * k].astype(F32) + recv_b[k].astype(F32)).astype(BF16)
         c_copy(k).start()
 
-    total = product(n - 1) + rows_ref[...].astype(F32)
+    total = product(n - 1) + gath[0].astype(F32)
     a_copy(0).wait_recv()
     b_copy(0).wait_recv()
     accum = total + recv_a[0].astype(F32) + recv_b[0].astype(F32)
@@ -346,15 +384,20 @@
     def _(k):
         c_copy(k).wait_recv()
 
-    hid_ref[...] = (accum + jnp.sum(recv_c[...].astype(F32), axis=0)).astype(BF16)
+    out = (accum + jnp.sum(recv_c[...].astype(F32), axis=0)).astype(BF16)
+    page_col = pages_ref[:, 0:1] * slots + pages_ref[:, 1:2]
+    pick = (lax.broadcasted_iota(jnp.int32, (per, per), 1) == page_col).astype(F32).astype(BF16)
+    for t in range(steps):
+        there = jnp.dot(pick, out[t * per : t * per + per], preferred_element_type=F32)
+        hid_ref[pl.ds(t * per, per), :] = there.astype(BF16)
 
     own_state_back.wait()
     own_conv_back.wait()
 
     @loop(1, n)
     def _(j):
-        state_back(j, xor(me, j)).wait_recv()
-        conv_back(j, xor(me, j)).wait_recv()
+        state_back(j, peer_of(j)).wait_recv()
+        conv_back(j, peer_of(j)).wait_recv()
         state_back(j, me).wait_send()
         conv_back(j, me).wait_send()
         state_copy(j, me).wait_send()
@@ -389,10 +432,7 @@
     dl = embedding.shape[1]
     rows = steps * per
     q = n // 4
-    page = page_table[:, 0] * slots + page_table[:, 1]
-    hit = page[:, None] == jnp.arange(per, dtype=page.dtype)[None]
-    paged = jnp.sum(jnp.where(hit[None], tokens[:, :, None], 0), axis=1)
-    local_rows = embedding[paged.reshape(-1)]
+    local_rows = embedding[tokens.reshape(-1)]
     width = proj_weight.shape[1]
     blocks = -(-width // LANES)
     tiles = -(-(rows // 16 * blocks) // n)
@@ -411,16 +451,16 @@
             jax.ShapeDtypeStruct(ssm_pages.shape, BF16),
             jax.ShapeDtypeStruct(conv_pages.shape, BF16),
         ),
-        in_specs=[vm] * 8 + [hbm] * 7,
+        in_specs=[vm] * 10 + [hbm] * 7,
         out_specs=(vm, hbm, hbm),
         scratch_shapes=[
-            V((n, dl, cl), BF16), V((n, dl, cl), BF16), V((n, cl, dl), BF16), V((cl, width), BF16), V((rank, cl), BF16),
+            V((n, dl, cl), BF16), V((n, dl, cl), BF16), V((n, cl, dl), BF16), V((width, cl), BF16), V((rank, cl), BF16),
             V((n, rows, dl), BF16), V((rows, cl), F32), V((rows, cl), F32), V((rows, 1), F32),
             V((n, slots, states, cl), BF16), V((n, slots, states, cl), BF16),
             V((n, slots, window, cl), BF16), V((n, slots, window, cl), BF16),
             V((window * per + rows, cl), F32), V((rows, cl), F32), V((rows, cl), F32), V((rows, cl), F32),
-            V((rows, blocks * LANES), F32), V((n, tiles, 16, LANES), BF16), V((n, tiles, 16, LANES), BF16),
-            V((tiles, 16, LANES), BF16), V((n, tiles, 16, LANES), BF16), V((rows, blocks * LANES), F32), V((rows, LANES), F32), V((rows, cl), BF16),
+            V((rows, blocks * LANES), F32), V((n, tiles, 16, LANES), SUM_TYPE), V((n, tiles, 16, LANES), SUM_TYPE),
+            V((tiles, 16, LANES), SUM_TYPE), V((n, tiles, 16, LANES), SUM_TYPE), V((rows, blocks * LANES), F32), V((rows, LANES), F32), V((rows, cl), BF16),
             V((n // 2, rows, dl), BF16), V((n // 2, rows, dl), BF16),
             V((q, rows, dl), BF16), V((q, rows, dl), BF16), V((q, rows, dl), BF16), V((q, rows, dl), BF16),
             dma((n,)), dma((n,)), dma((n,)), dma((4,)),
@@ -433,11 +473,18 @@
         ),
         cost_estimate=pl.CostEstimate(flops=2 * rows * cl * dl * n * 3, bytes_accessed=6 * cl * dl * n, transcendentals=0),
     )(
-        local_rows, norm_gain.reshape(n, 1, dl), conv_weight, conv_bias.reshape(1, cl), delta_gain.reshape(1, rank),
+        page_table, page_table.T, local_rows, norm_gain.reshape(n, 1, dl), conv_weight, conv_bias.reshape(1, cl), delta_gain.reshape(1, rank),
         delta_bias.reshape(1, cl), log_rates, skip_gain.reshape(1, cl),
-        x_weight, z_weight, proj_weight, delta_weight, out_w, ssm_pages, conv_pages,
+        x_weight, z_weight, proj_weight.T, delta_weight, out_w, ssm_pages, conv_pages,
     )
-    return hid.reshape(steps, per, dl)[:, page], ssm_out, conv_out
+    hid, ssm_out, conv_out = pl.pallas_call(
+        hand_on,
+        out_shape=tuple(jax.ShapeDtypeStruct(v.shape, v.dtype) for v in (hid, ssm_out, conv_out)),
+        in_specs=[hbm] * 3,
+        out_specs=(hbm,) * 3,
+        scratch_shapes=[dma((PIECES + 2,))],
+    )(hid, ssm_out, conv_out)
+    return hid.reshape(steps, per, dl), ssm_out, conv_out
 
 
 def solution(mesh):

time: 79.1 us -> 90.3 us (1.14)
  Pallas kernels: 65.7 us -> 84.6 us
  local copies, waits for them, and re-layouts: 10.7 us -> 4.8 us
  other arithmetic: 1.63 us -> 0.01 us
    pallas_call x0 -> x1, Pallas kernels: none -> 22.5 us  [body(): pl.pallas_call(hand_on, out_shape=tuple((jax.ShapeDtypeStruct(v.shape, v....]
    unnamed x4 -> x1, local copies, waits for them, and re-layouts: 6.52 us -> 1.35 us
    pallas_call x1, Pallas kernels: 65.7 us -> 62.1 us  [body(): pl.pallas_call(functools.partial(kernel, n, steps, slots, rank, states),...]
    gather x2 -> x1, local copies, waits for them, and re-layouts: 3.3 us -> 2.68 us  [body(): local_rows = embedding[tokens.reshape(-1)]]
where the time goes in v2:
time: 90.3 us; the launch traced here: 90 us
  Pallas kernels  84.6 us (94%)
  local copies, waits for them, and re-layouts  4.8 us (5%)
    pallas_call x1, Pallas kernels, body(): pl.pallas_call(functools.partial(kernel, n, steps, slots, rank, states),...  62.1 us
    pallas_call x1, Pallas kernels, body(): pl.pallas_call(hand_on, out_shape=tuple((jax.ShapeDtypeStruct(v.shape, v....  22.5 us
    gather x1, local copies, waits for them, and re-layouts, body(): local_rows = embedding[tokens.reshape(-1)]  2.68 us

profile of v2, /device:TPU:0, one launch (start us, length us, event | category | flops | bytes accessed | tf_op | source)
XLA Modules:
  0.0 90.0 jit_solution(16482050910441054055)
XLA Ops:
  0.6 0.8 reshape.55
  1.4 1.4 %copy.20.pages_ref = s32[16,2]{1,0:T(8,128)} copy(s32[16,2]{0,1:T(2,128)} %param.18) | data formatting | bytes 256 | tf_op args[1]
  2.8 2.7 %gather_fusion = bf16[48,512]{1,0:T(8,128)(2,1)} fusion(bf16[32768,512]{1,0:T(8,128)(2,1)} %param.19, s32[1024]{0:T(1024)S(1)} %pad_clamp_fusion), kind=kCustom, calls=%fused_computation | custom fusion | bytes 98496 | tf_op jit(solution)/shard_map/gather | solution.py:435
  5.4 62.1 %shard_map.184 = (bf16[48,512]{1,0:T(8,128)(2,1)}, bf16[1,16,16384]{2,1,0:T(8,128)(2,1)}, bf16[1,3,16384]{2,1,0:T(4,128)(2,1)}) custom-call(s32[16,2]{1,0:T(8,128)} %copy.20.pages_ref, s32[2,16]{1,0:T(2,128)} %bitcast.12, bf16[48,512]{1,0:T(8,128)(2,1)} %gather_fusion, f32[16,1,512]{2,1,0:T(1,128)} %bitcast.11, f32[4,1024]{1,0:T(4,128)} %conv_w_ref.1, ...), custom_call_target="tpu_custom_call" | custom-call | flops 2415919104 | bytes 50331648 | tf_op jit(solution)/shard_map/pallas_call | solution.py:447
  67.5 22.5 %shard_map.185 = (bf16[48,512]{1,0:T(8,128)(2,1)}, bf16[1,16,16384]{2,1,0:T(8,128)(2,1)}, bf16[1,3,16384]{2,1,0:T(4,128)(2,1)}) custom-call(bf16[48,512]{1,0:T(8,128)(2,1)} %get-tuple-element.9.hid, bf16[1,16,16384]{2,1,0:T(8,128)(2,1)} %get-tuple-element.10.ssm, bf16[1,3,16384]{2,1,0:T(4,128)(2,1)} %get-tuple-element.11.conv), custom_call_target="tpu_custom_call" | custom-call | tf_op jit(solution)/shard_map/pallas_call | solution.py:480
  (2 shorter events, 0.0 us)

commit v3 on v2

--- a/solution.py
+++ b/solution.py
@@ -18,23 +18,27 @@
     return 1.0 / (1.0 + jnp.exp(-v))
 
 
-def hand_on(hid, ssm, conv, hid_to, ssm_to, conv_to, sems):
+def hand_on(hid, ssm, conv, hid_to, ssm_to, conv_to, hid_v, ssm_v, conv_v, sems):
     wide = ssm.shape[2] // PIECES
-    copies = [
-        pltpu.make_async_copy(ssm.at[:, :, k * wide : k * wide + wide], ssm_to.at[:, :, k * wide : k * wide + wide], sems.at[k])
+    hops = [
+        (ssm.at[:, :, k * wide : k * wide + wide], ssm_v.at[k], ssm_to.at[:, :, k * wide : k * wide + wide])
         for k in range(PIECES)
     ]
-    copies.append(pltpu.make_async_copy(conv, conv_to, sems.at[PIECES]))
-    copies.append(pltpu.make_async_copy(hid, hid_to, sems.at[PIECES + 1]))
-    for copy in copies:
+    hops += [(conv, conv_v, conv_to), (hid, hid_v, hid_to)]
+    into = [pltpu.make_async_copy(a, b, sems.at[0, k]) for k, (a, b, _) in enumerate(hops)]
+    away = [pltpu.make_async_copy(b, c, sems.at[1, k]) for k, (_, b, c) in enumerate(hops)]
+    for copy in into:
         copy.start()
-    for copy in copies:
+    for first, second in zip(into, away):
+        first.wait()
+        second.start()
+    for copy in away:
         copy.wait()
 
 
 def kernel(
     n, steps, slots, rank, states,
-    pages_ref, paged_ref, rows_ref, gain_ref, conv_w_ref, conv_b_ref, dgain_ref, dbias_ref, lograte_ref, skip_ref,
+    paged_ref, rows_ref, gain_ref, conv_w_ref, conv_b_ref, dgain_ref, dbias_ref, lograte_ref, skip_ref,
     xw_hbm, zw_hbm, proj_hbm, dw_hbm, ow_hbm, ssm_hbm, conv_hbm,
     hid_ref, ssm_out, conv_out,
     xw, zw, ow, pw, dw,
@@ -385,8 +389,11 @@
         c_copy(k).wait_recv()
 
     out = (accum + jnp.sum(recv_c[...].astype(F32), axis=0)).astype(BF16)
-    page_col = pages_ref[:, 0:1] * slots + pages_ref[:, 1:2]
-    pick = (lax.broadcasted_iota(jnp.int32, (per, per), 1) == page_col).astype(F32).astype(BF16)
+    ids = jnp.broadcast_to((paged_ref[0:1, :] * slots + paged_ref[1:2, :]).astype(F32), (per, per))
+    across = lax.broadcasted_iota(jnp.int32, (per, per), 1)
+    down = lax.broadcasted_iota(jnp.int32, (per, per), 0)
+    page_col = jnp.sum(jnp.where(across == down, ids, 0.0), axis=1, keepdims=True)
+    pick = (across.astype(F32) == page_col).astype(F32).astype(BF16)
     for t in range(steps):
         there = jnp.dot(pick, out[t * per : t * per + per], preferred_element_type=F32)
         hid_ref[pl.ds(t * per, per), :] = there.astype(BF16)
@@ -451,7 +458,7 @@
             jax.ShapeDtypeStruct(ssm_pages.shape, BF16),
             jax.ShapeDtypeStruct(conv_pages.shape, BF16),
         ),
-        in_specs=[vm] * 10 + [hbm] * 7,
+        in_specs=[vm] * 9 + [hbm] * 7,
         out_specs=(vm, hbm, hbm),
         scratch_shapes=[
             V((n, dl, cl), BF16), V((n, dl, cl), BF16), V((n, cl, dl), BF16), V((width, cl), BF16), V((rank, cl), BF16),
@@ -473,7 +480,7 @@
         ),
         cost_estimate=pl.CostEstimate(flops=2 * rows * cl * dl * n * 3, bytes_accessed=6 * cl * dl * n, transcendentals=0),
     )(
-        page_table, page_table.T, local_rows, norm_gain.reshape(n, 1, dl), conv_weight, conv_bias.reshape(1, cl), delta_gain.reshape(1, rank),
+        page_table.T, local_rows, norm_gain.reshape(n, 1, dl), conv_weight, conv_bias.reshape(1, cl), delta_gain.reshape(1, rank),
         delta_bias.reshape(1, cl), log_rates, skip_gain.reshape(1, cl),
         x_weight, z_weight, proj_weight.T, delta_weight, out_w, ssm_pages, conv_pages,
     )
@@ -482,7 +489,10 @@
         out_shape=tuple(jax.ShapeDtypeStruct(v.shape, v.dtype) for v in (hid, ssm_out, conv_out)),
         in_specs=[hbm] * 3,
         out_specs=(hbm,) * 3,
-        scratch_shapes=[dma((PIECES + 2,))],
+        scratch_shapes=[
+            V(hid.shape, BF16), V((PIECES, slots, states, ssm_out.shape[2] // PIECES), BF16), V(conv_out.shape, BF16),
+            dma((2, PIECES + 2)),
+        ],
     )(hid, ssm_out, conv_out)
     return hid.reshape(steps, per, dl), ssm_out, conv_out
 

time: 90.3 us -> 68.4 us (0.76)
  Pallas kernels: 84.6 us -> 64 us
  local copies, waits for them, and re-layouts: 4.8 us -> 3.43 us
    pallas_call x1, Pallas kernels: 22.5 us -> 1.93 us  [body(): pl.pallas_call(hand_on, out_shape=tuple((jax.ShapeDtypeStruct(v.shape, v....]
    unnamed x1 -> x0, local copies, waits for them, and re-layouts: 1.35 us -> none
where the time goes in v3:
time: 68.4 us; the launch traced here: 68.1 us
  Pallas kernels  64 us (94%)
  local copies, waits for them, and re-layouts  3.43 us (5%)
    pallas_call x1, Pallas kernels, body(): pl.pallas_call(functools.partial(kernel, n, steps, slots, rank, states),...  62.1 us
    gather x1, local copies, waits for them, and re-layouts, body(): local_rows = embedding[tokens.reshape(-1)]  2.67 us
    pallas_call x1, Pallas kernels, body(): pl.pallas_call(hand_on, out_shape=tuple((jax.ShapeDtypeStruct(v.shape, v....  1.93 us

profile of v3, /device:TPU:0, one launch (start us, length us, event | category | flops | bytes accessed | tf_op | source)
XLA Modules:
  0.0 68.1 jit_solution(11086575659608351303)
XLA Ops:
  0.6 0.8 %reshape.55 = s32[48,1]{0,1:T(1,128)S(1)} reshape(s32[3,16]{1,0:T(4,128)} %param.17) | data formatting | bytes 384 | tf_op jit(solution)/shard_map/reshape | solution.py:442
  1.4 2.7 %gather_fusion = bf16[48,512]{1,0:T(8,128)(2,1)} fusion(bf16[32768,512]{1,0:T(8,128)(2,1)} %param.19, s32[1024]{0:T(1024)S(1)} %pad_clamp_fusion), kind=kCustom, calls=%fused_computation | custom fusion | bytes 98496 | tf_op jit(solution)/shard_map/gather | solution.py:442
  4.1 62.1 %shard_map.184 = (bf16[48,512]{1,0:T(8,128)(2,1)}, bf16[1,16,16384]{2,1,0:T(8,128)(2,1)}, bf16[1,3,16384]{2,1,0:T(4,128)(2,1)}) custom-call(s32[2,16]{1,0:T(2,128)} %bitcast.16, bf16[48,512]{1,0:T(8,128)(2,1)} %gather_fusion, f32[16,1,512]{2,1,0:T(1,128)} %bitcast.11, f32[4,1024]{1,0:T(4,128)} %conv_w_ref.1, f32[1,1024]{1,0:T(1,128)} %bitcast.12, ...), custom_call_target="tpu_custom_call" | custom-call | flops 2415919104 | bytes 50331648 | tf_op jit(solution)/shard_map/pallas_call | solution.py:454
  66.2 1.9 %shard_map.185 = (bf16[48,512]{1,0:T(8,128)(2,1)}, bf16[1,16,16384]{2,1,0:T(8,128)(2,1)}, bf16[1,3,16384]{2,1,0:T(4,128)(2,1)}) custom-call(bf16[48,512]{1,0:T(8,128)(2,1)} %get-tuple-element.9.hid, bf16[1,16,16384]{2,1,0:T(8,128)(2,1)} %get-tuple-element.10.ssm, bf16[1,3,16384]{2,1,0:T(4,128)(2,1)} %get-tuple-element.11.conv), custom_call_target="tpu_custom_call" | custom-call | tf_op jit(solution)/shard_map/pallas_call | solution.py:487
  (2 shorter events, 0.0 us)
